TPU v7x, 32 devices: a whole 2x2x4 slice. The times are simulated.
32 devices in a mesh: row: 4 (over z), col: 8 (over y, x, core).
Axes of the slice: x: 2, y: 2, z: 4, core: 2. Of those that a mesh axis runs over, the one named last changes fastest.
Arguments:
- trail_adjoint: float32 [4096, 4096], P('row', 'col'), may hold values from -0.09375 to 0.09375
- panel: float32 [4096, 128], P('row', 'col')
- panel_adjoint: float32 [4096, 128], P('row', 'col'), may hold values from -6 to 6
- inv_diag: float32 [128, 128], replicated, as said below
- panel_index: int32 [1], replicated, may hold values from 832 to 895
Outputs:
- panel_grad: float32 [4096, 128], P('row', 'col')
- diag_grad: float32 [128, 128], P(None, 'col')
Inputs may be any that keep to these rules, and one draw needn't show every extreme that they name: inv_diag is lower triangular with a positive diagonal.
All inputs are finite; a program needn't handle non-finite values.
Results may differ from a plain program's by a relative error of at most 0.000075.
Values sent between devices are 32-bit elements; how exact they have to be, the bound alone decides.
A program may use at most 64 MiB of HBM per device.

v0:
```python
import jax
import jax.numpy as jnp
from jax import lax
from jax.sharding import PartitionSpec as P


def broadcast(value, axis, root):
    mine = lax.axis_index(axis) == root
    return lax.psum(jnp.where(mine, value, jnp.zeros_like(value)), axis)


def body(trail_adjoint, panel, panel_adjoint, inv_diag, panel_index):
    rows_here, thin_cols = panel.shape
    panel_width = inv_diag.shape[0]
    ways_row = lax.axis_size("row")
    ways_col = lax.axis_size("col")
    ways_ratio = ways_col // ways_row
    col_here = lax.axis_index("col")
    index_k = panel_index[0]
    start_mod = jnp.mod(col_here - index_k - 1, ways_col)
    offset = start_mod // ways_row
    col_blocks = rows_here // (panel_width * ways_ratio)
    root_row = jnp.mod(col_here, ways_row)
    panel_rows = lax.all_gather(panel, "col", axis=1, tiled=True)
    shaped = broadcast(panel_rows, "row", root_row).reshape(
        col_blocks, ways_ratio, panel_width, panel_width
    )
    chosen = lax.dynamic_slice_in_dim(shaped, offset, 1, 1)
    column_panel = chosen.reshape(col_blocks * panel_width, panel_width)
    product = jnp.dot(
        trail_adjoint,
        column_panel,
        precision=lax.Precision.HIGHEST,
        preferred_element_type=jnp.float32,
    )
    placed = lax.dynamic_update_slice_in_dim(
        jnp.zeros((rows_here, panel_width), jnp.float32), panel_adjoint, col_here * thin_cols, 1
    )
    local_term = placed - 2.0 * product
    my_inverse = lax.dynamic_slice_in_dim(inv_diag, col_here * thin_cols, thin_cols, 1)
    contract_rows = (((0,), (0,)), ((), ()))
    thin_part = lax.psum_scatter(local_term, "col", scatter_dimension=1, tiled=True)
    full_rows = lax.all_gather(thin_part, "col", axis=1, tiled=True)
    panel_grad = jnp.dot(
        full_rows, my_inverse, precision=lax.Precision.HIGHEST, preferred_element_type=jnp.float32
    )
    gram_local = lax.dot_general(
        full_rows,
        panel,
        contract_rows,
        precision=lax.Precision.HIGHEST,
        preferred_element_type=jnp.float32,
    )
    gram_total = lax.psum(gram_local, "row")
    diag_grad = -lax.dot_general(
        inv_diag,
        gram_total,
        contract_rows,
        precision=lax.Precision.HIGHEST,
        preferred_element_type=jnp.float32,
    )
    return (panel_grad, diag_grad)


def solution(mesh):
    in_specs = (P("row", "col"), P("row", "col"), P("row", "col"), P(), P())
    out_specs = (P("row", "col"), P(None, "col"))
    return jax.shard_map(body, mesh=mesh, in_specs=in_specs, out_specs=out_specs, check_vma=False)
```

profile of v0, /device:TPU:0, one launch (start us, length us, event | category | flops | bytes accessed | tf_op | source)
XLA Modules:
  0.0 137.0 jit_solution(3447076035623362426)
XLA Ops:
  7.2 0.0 copy-start
  7.2 0.0 copy-start.3
  7.2 0.0 all-reduce.2.cloned.1.call-start
  7.2 11.7 %all_gather.6 = f32[1024,128]{0,1:T(8,128)S(1)} all-gather(f32[1024,16]{0,1:T(8,128)} %param.6), channel_id=1, replica_groups=mesh['row'=4,'col'=8] {'col'}, dimensions={1}, use_global_device_ids=true | all-gather | bytes 589824 | tf_op jit(solution)/shard_map/all_gather | solution.py:24
  19.0 1.3 reshape.10
  20.3 0.0 all-reduce.2.cloned.1.call-update
  20.3 0.0 reduce-scatter.2.cloned.1.call-start
  21.1 0.0 copy-done.3
  21.1 37.9 %all-reduce.2.cloned.1.call-done = f32[4,2,128,128]{2,1,0,3:T(2,128)} async-done(((f32[4,2,128,128]{2,1,0,3:T(2,128)}), f32[4,2,128,128]{2,1,0,3:T(2,128)}) %all-reduce.2.cloned.1.call-update) | async-done | bytes 524304 | tf_op jit(solution)/shard_map/psum | solution.py:9
  59.0 1.9 %dynamic-slice_reduce_fusion = f32[4,128,128]{1,0,2:T(4,128)S(1)} fusion(f32[4,2,128,128]{2,1,0,3:T(2,128)} %all-reduce.2.cloned.1.call-done, s32[]{:T(128)S(6)} %select_n.36), kind=kLoop, calls=%fused_computation.7 | loop fusion | bytes 524292 | tf_op jit(solution)/shard_map/dynamic_slice | solution.py:28
  60.9 0.0 copy-done
  60.9 0.0 copy-start.1
  60.9 0.0 copy-start.2
  60.9 3.1 %fusion.1 = f32[1024,128]{0,1:T(8,128)} fusion(f32[1024,128]{0,1:T(8,128)S(1)} %constant_dynamic-update-slice_fusion, f32[1024,512]{1,0:T(8,128)S(1)} %copy-done, f32[16,8,4,128]{3,2,1,0:T(4,128)S(1)} %bitcast.22), kind=kOutput, calls=%fused_computation.2 | convolution fusion | flops 805568512 | bytes 3407872 | tf_op jit(solution)/shard_map/dot_general | solution.py:30
  64.0 0.0 reduce-scatter.2.cloned.1.call-update
  64.0 34.2 %reduce-scatter.2.cloned.1.call-done = f32[1024,16]{0,1:T(8,128)} async-done(((f32[1024,128]{0,1:T(8,128)}), f32[1024,16]{0,1:T(8,128)}) %reduce-scatter.2.cloned.1.call-update) | async-done | bytes 65552 | tf_op jit(solution)/shard_map/reduce_scatter | solution.py:42
  98.3 9.8 %all_gather.7 = f32[1024,128]{0,1:T(8,128)S(1)} all-gather(f32[1024,16]{0,1:T(8,128)} %reduce-scatter.2.cloned.1.call-done), channel_id=1, replica_groups=mesh['row'=4,'col'=8] {'col'}, dimensions={1}, use_global_device_ids=true | all-gather | bytes 589824 | tf_op jit(solution)/shard_map/all_gather | solution.py:43
  108.0 0.0 copy-done.1
  108.1 0.5 fusion.8
  108.6 0.0 copy-done.2
  108.6 1.1 fusion.5
  109.7 19.6 %psum.15 = f32[128,16]{1,0:T(8,128)S(1)} all-reduce(f32[128,16]{1,0:T(8,128)S(1)} %fusion.8), channel_id=1, replica_groups=mesh['row'=4,'col'=8] {'row'}, use_global_device_ids=true, to_apply=%region_2.3 | all-reduce | flops 2048 | bytes 16384 | tf_op jit(solution)/shard_map/psum | solution.py:54
  129.3 0.9 fusion.2
  (3 shorter events, 0.1 us)
Async XLA Ops:
  7.2 53.7 %copy-start = (f32[1024,512]{1,0:T(8,128)S(1)}, f32[1024,512]{1,0:T(8,128)}, u32[]{:S(2)}) copy-start(f32[1024,512]{1,0:T(8,128)} %param.5) | copy-start | bytes 6291460
  7.2 13.9 %copy-start.3 = (f32[1024,16]{0,1:T(8,128)S(1)}, f32[1024,16]{0,1:T(8,128)}, u32[]{:S(2)}) copy-start(f32[1024,16]{0,1:T(8,128)} %param.7) | copy-start | bytes 196612
  7.2 51.8 %all-reduce.2.cloned.1.call-start = ((), (), s32[]{:S(2)}) async-start(), calls=%async_computation.1 | async-start | bytes 1048576 | tf_op jit(solution)/shard_map/psum | solution.py:9
  20.3 78.0 %reduce-scatter.2.cloned.1.call-start = ((), (), s32[]{:S(2)}) async-start(), calls=%async_computation.2 | async-start | bytes 589824 | tf_op jit(solution)/shard_map/reduce_scatter | solution.py:42
  60.9 47.2 %copy-start.1 = (f32[1024,16]{0,1:T(8,128)S(1)}, f32[1024,16]{0,1:T(8,128)}, u32[]{:S(2)}) copy-start(f32[1024,16]{0,1:T(8,128)} %param.6) | copy-start | bytes 196612
  60.9 47.7 %copy-start.2 = (f32[128,128]{1,0:T(8,128)S(1)}, f32[128,128]{1,0:T(8,128)}, u32[]{:S(2)}) copy-start(f32[128,128]{1,0:T(8,128)} %param.8) | copy-start | bytes 196612
Sparse Core Ops, SparseCore 0:
  20.4 38.5 all-reduce.1
  64.2 34.0 reduce-scatter.1
where the time goes:
time: 137 us
  waiting for transfers between devices  72.2 us (53%)
  blocking collectives  41.1 us (30%)
  between operations  14.8 us (11%)
  matrix products  5.56 us (4%)
  local copies, waits for them, and re-layouts  3.19 us (2%)
    psum x1, waiting for transfers between devices, broadcast(): return lax.psum(jnp.where(mine, value, jnp.zeros_like(value)), axis)  37.9 us
    reduce_scatter x1, waiting for transfers between devices, body(): lax.psum_scatter(local_term, 'col', scatter_dimension=1, tiled=True)  34.2 us
    psum x1, blocking collectives, body(): gram_total = lax.psum(gram_local, 'row')  19.6 us
    all_gather x1, blocking collectives, body(): panel_rows = lax.all_gather(panel, 'col', axis=1, tiled=True)  11.7 us
    all_gather x1, blocking collectives, body(): full_rows = lax.all_gather(thin_part, 'col', axis=1, tiled=True)  9.78 us
    dot_general x1, matrix products, body(): jnp.dot(trail_adjoint, column_panel, precision=lax.Precision.HIGHEST, pre...  3.08 us
  transfers between devices with their start and end apart: 2, of which 2 were waited for; matrix products, arithmetic and copies ran while one was open for 0% of the time, Pallas kernels for 0%

commit v1 on v0

--- a/solution.py
+++ b/solution.py
@@ -1,7 +1,13 @@
+import functools
+
 import jax
 import jax.numpy as jnp
 from jax import lax
+from jax.experimental import pallas as pl
+from jax.experimental.pallas import tpu as pltpu
 from jax.sharding import PartitionSpec as P
+
+MESH = pl.DeviceIdType.MESH
 
 
 def broadcast(value, axis, root):
@@ -62,7 +68,222 @@
     return (panel_grad, diag_grad)
 
 
+def split(value):
+    high = value.astype(jnp.bfloat16)
+    return high, (value - high.astype(jnp.float32)).astype(jnp.bfloat16)
+
+
+def dot(a, b, dims):
+    return lax.dot_general(a, b, (dims, ((), ())), preferred_element_type=jnp.float32)
+
+
+def kernel(
+    n_row, n_col, idx_ref, trail_ref, panel_ref, adj_ref, inv_ref, grad_ref, diag_ref,
+    trail_v, t_hi, t_lo, base, z_buf, p_full, stage, cp_buf, q_buf, q_in, d_buf, d_in, d_z,
+    t_sem, z_send, z_recv, p_send, p_recv, c_send, c_recv, q_send, q_recv, d_send, d_recv, dz_send, dz_recv,
+):
+    thin, rows = panel_ref.shape
+    width = inv_ref.shape[0]
+    cols = trail_ref.shape[1]
+    ratio = n_col // n_row
+    my_row, my_col = lax.axis_index("row"), lax.axis_index("col")
+
+    load = pltpu.make_async_copy(trail_ref, trail_v, t_sem)
+    load.start()
+
+    def row_at(shift):
+        return {"row": lax.rem(my_row + shift, n_row)}
+
+    def col_at(shift):
+        return {"col": lax.rem(my_col + shift, n_col)}
+
+    def col_from(shift):
+        return lax.rem(my_col + n_col - shift, n_col)
+
+    barrier = pltpu.get_barrier_semaphore()
+    for shift in range(1, n_row):
+        pl.semaphore_signal(barrier, inc=1, device_id=row_at(shift), device_id_type=MESH)
+    for shift in range(1, n_col):
+        pl.semaphore_signal(barrier, inc=1, device_id=col_at(shift), device_id_type=MESH)
+    pl.semaphore_wait(barrier, n_row + n_col - 2)
+
+    def remote(src, dst, send, recv, where):
+        return pltpu.make_async_remote_copy(
+            src_ref=src, dst_ref=dst, send_sem=send, recv_sem=recv, device_id=where, device_id_type=MESH
+        )
+
+    z_copies = [
+        remote(panel_ref, z_buf.at[s], z_send.at[s], z_recv.at[s], row_at(s)) for s in range(1, n_row)
+    ]
+    for copy in z_copies:
+        copy.start()
+    p_copies = [
+        remote(panel_ref, p_full.at[my_col], p_send.at[s], p_recv.at[s], col_at(s)) for s in range(1, n_col)
+    ]
+
+    index_k = idx_ref[0]
+
+    def forward(shift):
+        piece = panel_ref[...] if shift == 0 else z_buf[shift]
+        source = lax.rem(my_row + n_row - shift, n_row)
+        for group in range(ratio):
+            target = source + n_row * group
+            offset = jnp.mod(target - index_k - 1, n_col) // n_row
+            slot = shift * ratio + group
+            for block in range(rows // (width * ratio)):
+                at = block * ratio * width
+                part = piece[:, at : at + width]
+                for other in range(1, ratio):
+                    part = jnp.where(
+                        offset == other, piece[:, at + other * width : at + (other + 1) * width], part
+                    )
+                stage[slot, :, block * width : (block + 1) * width] = part
+            away = lax.rem(target + n_col - my_col, n_col)
+
+            @pl.when(away != 0)
+            def _():
+                remote(
+                    stage.at[slot], cp_buf.at[my_col], c_send.at[away], c_recv.at[away], {"col": target}
+                ).start()
+
+            @pl.when(away == 0)
+            def _():
+                cp_buf[my_col] = stage[slot]
+
+    forward(0)
+    for copy in p_copies:
+        copy.start()
+    p_full[my_col] = panel_ref[...]
+
+    adj_hi, adj_lo = split(adj_ref[...])
+    inv_hi, inv_lo = split(inv_ref[pl.ds(pl.multiple_of(my_col * thin, 8), thin), :])
+    base[...] = dot(
+        jnp.concatenate([inv_hi, inv_lo, inv_hi], 0), jnp.concatenate([adj_hi, adj_hi, adj_lo], 0), ((0,), (0,))
+    )
+    load.wait()
+    trail_t = trail_v[...].T
+    hi, lo = split(trail_t)
+    t_hi[...] = hi
+    t_lo[...] = lo
+
+    for shift in range(1, n_row):
+        z_copies[shift - 1].wait_recv()
+        forward(shift)
+
+    inv_hi, inv_lo = split(inv_ref[...].T)
+    for s in range(1, n_col):
+        where = cp_buf.at[col_from(s)]
+        remote(where, where, c_send.at[s], c_recv.at[s], col_at(s)).wait_recv()
+    cp_hi, cp_lo = split(cp_buf[...].reshape(width, cols))
+    w = -2.0 * dot(
+        jnp.concatenate([inv_hi, inv_lo, inv_hi], 1), jnp.concatenate([cp_hi, cp_hi, cp_lo], 0), ((1,), (0,))
+    )
+    w_hi, w_lo = split(w)
+    both = dot(jnp.concatenate([w_hi, w_lo], 0), t_hi[...], ((1,), (0,)))
+    q = base[...] + both[:width] + both[width:] + dot(w_hi, t_lo[...], ((1,), (0,)))
+    q_buf[...] = q.reshape(n_col, thin, rows)
+    q_copies = []
+    for s in range(1, n_col):
+        copy = remote(
+            q_buf.at[lax.rem(my_col + s, n_col)], q_in.at[s], q_send.at[s], q_recv.at[s], col_at(s)
+        )
+        copy.start()
+        q_copies.append(copy)
+
+    for s in range(1, n_col):
+        where = p_full.at[col_from(s)]
+        remote(where, where, p_send.at[s], p_recv.at[s], col_at(s)).wait_recv()
+    q_hi, q_lo = split(q)
+    f_hi, f_lo = split(p_full[...].reshape(width, rows))
+    nt = ((1,), (1,))
+    d = -(dot(f_hi, q_hi, nt) + dot(f_hi, q_lo, nt) + dot(f_lo, q_hi, nt))
+    d_buf[...] = d.reshape(n_col, thin, width)
+    d_copies = []
+    for s in range(1, n_col):
+        copy = remote(
+            d_buf.at[lax.rem(my_col + s, n_col)], d_in.at[s], d_send.at[s], d_recv.at[s], col_at(s)
+        )
+        copy.start()
+        d_copies.append(copy)
+    total = d_buf[my_col]
+    for s in range(1, n_col):
+        d_copies[s - 1].wait_recv()
+        total = total + d_in[s]
+    d_z[my_row] = total
+    dz_copies = []
+    for s in range(1, n_row):
+        copy = remote(d_z.at[my_row], d_z.at[my_row], dz_send.at[s], dz_recv.at[s], row_at(s))
+        copy.start()
+        dz_copies.append(copy)
+
+    total = q_buf[my_col]
+    for s in range(1, n_col):
+        q_copies[s - 1].wait_recv()
+        total = total + q_in[s]
+    grad_ref[...] = total
+
+    for s in range(1, n_row):
+        where = d_z.at[lax.rem(my_row + n_row - s, n_row)]
+        remote(where, where, dz_send.at[s], dz_recv.at[s], row_at(s)).wait_recv()
+    total = d_z[0]
+    for r in range(1, n_row):
+        total = total + d_z[r]
+    diag_ref[...] = total
+
+    for s in range(1, n_col):
+        remote(stage.at[0], cp_buf.at[my_col], c_send.at[s], c_recv.at[s], col_at(s)).wait_send()
+    for copy in z_copies + p_copies + q_copies + d_copies + dz_copies:
+        copy.wait_send()
+
+
+def fused(trail_adjoint, panel, panel_adjoint, inv_diag, panel_index):
+    rows, thin = panel.shape
+    cols = trail_adjoint.shape[1]
+    width = inv_diag.shape[0]
+    n_row, n_col = lax.axis_size("row"), lax.axis_size("col")
+    f32, bf16 = jnp.float32, jnp.bfloat16
+    vmem = pl.BlockSpec(memory_space=pltpu.VMEM)
+    dma = pltpu.SemaphoreType.DMA
+    grad, diag = pl.pallas_call(
+        functools.partial(kernel, n_row, n_col),
+        out_shape=(jax.ShapeDtypeStruct((thin, rows), f32), jax.ShapeDtypeStruct((thin, width), f32)),
+        in_specs=[pl.BlockSpec(memory_space=pltpu.SMEM), pl.BlockSpec(memory_space=pl.ANY), vmem, vmem, vmem],
+        out_specs=(vmem, vmem),
+        scratch_shapes=[
+            pltpu.VMEM((rows, cols), f32),
+            pltpu.VMEM((cols, rows), bf16),
+            pltpu.VMEM((cols, rows), bf16),
+            pltpu.VMEM((width, rows), f32),
+            pltpu.VMEM((n_row, thin, rows), f32),
+            pltpu.VMEM((n_col, thin, rows), f32),
+            pltpu.VMEM((n_col, thin, cols), f32),
+            pltpu.VMEM((n_col, thin, cols), f32),
+            pltpu.VMEM((n_col, thin, rows), f32),
+            pltpu.VMEM((n_col, thin, rows), f32),
+            pltpu.VMEM((n_col, thin, width), f32),
+            pltpu.VMEM((n_col, thin, width), f32),
+            pltpu.VMEM((n_row, thin, width), f32),
+            dma,
+            dma((n_row,)), dma((n_row,)),
+            dma((n_col,)), dma((n_col,)),
+            dma((n_col,)), dma((n_col,)),
+            dma((n_col,)), dma((n_col,)),
+            dma((n_col,)), dma((n_col,)),
+            dma((n_row,)), dma((n_row,)),
+        ],
+        compiler_params=pltpu.CompilerParams(
+            collective_id=0, has_side_effects=True, vmem_limit_bytes=40 * 2**20
+        ),
+    )(panel_index, trail_adjoint, panel.T, panel_adjoint.T, inv_diag)
+    return grad.T, diag.T
+
+
+def choose(trail_adjoint, panel, panel_adjoint, inv_diag, panel_index):
+    step = fused if panel.shape[1] % 8 == 0 else body
+    return step(trail_adjoint, panel, panel_adjoint, inv_diag, panel_index)
+
+
 def solution(mesh):
     in_specs = (P("row", "col"), P("row", "col"), P("row", "col"), P(), P())
     out_specs = (P("row", "col"), P(None, "col"))
-    return jax.shard_map(body, mesh=mesh, in_specs=in_specs, out_specs=out_specs, check_vma=False)
+    return jax.shard_map(choose, mesh=mesh, in_specs=in_specs, out_specs=out_specs, check_vma=False)

time: 137 us -> 36.2 us (0.26)
  waiting for transfers between devices: 72.2 us -> 0 us
  blocking collectives: 41.1 us -> 0 us
  Pallas kernels: 0 us -> 29.2 us
  between operations: 14.8 us -> 1.3 us
  matrix products: 5.56 us -> 0 us
  local copies, waits for them, and re-layouts: 3.19 us -> 5.33 us
    psum x1 -> x0, waiting for transfers between devices: 37.9 us -> none  [broadcast(): return lax.psum(jnp.where(mine, value, jnp.zeros_like(value)), axis)]
    reduce_scatter x1 -> x0, waiting for transfers between devices: 34.2 us -> none  [body(): lax.psum_scatter(local_term, 'col', scatter_dimension=1, tiled=True)]
    pallas_call x0 -> x1, Pallas kernels: none -> 29.2 us  [fused(): pl.pallas_call(functools.partial(kernel, n_row, n_col), out_shape=(jax.Sh...]
    all_gather x2 -> x0, blocking collectives: 21.5 us -> none  [the longest x1 11.7 us: body(): panel_rows = lax.all_gather(panel, 'col', axis=1, tiled=True)]
    psum x1 -> x0, blocking collectives: 19.6 us -> none  [body(): gram_total = lax.psum(gram_local, 'row')]
    dot_general x4 -> x0, matrix products: 5.56 us -> none  [the longest x1 3.08 us: body(): jnp.dot(trail_adjoint, column_panel, precision=lax.Precision.HIGHEST, pre...]
    unnamed x8 -> x10, local copies, waits for them, and re-layouts: 0.03 us -> 5.33 us
    dynamic_slice x1 -> x0, local copies, waits for them, and re-layouts: 1.85 us -> none  [body(): chosen = lax.dynamic_slice_in_dim(shaped, offset, 1, 1)]
  transfers between devices with their start and end apart: 2 -> 0, of which waited for: 2 -> 0; matrix products, arithmetic and copies ran while one was open for 0% -> 0% of each run, Pallas kernels for 0% -> 0%
where the time goes in v1:
time: 36.2 us; the launch traced here: 35.8 us
  Pallas kernels  29.2 us (81%)
  local copies, waits for them, and re-layouts  5.33 us (15%)
  between operations  1.3 us (4%)
    pallas_call x1, Pallas kernels, fused(): pl.pallas_call(functools.partial(kernel, n_row, n_col), out_shape=(jax.Sh...  29.2 us
    unnamed x10, local copies, waits for them, and re-layouts  5.33 us

profile of v1, /device:TPU:0, one launch (start us, length us, event | category | flops | bytes accessed | tf_op | source)
XLA Modules:
  0.0 35.8 jit_solution(10076245465948325876)
XLA Ops:
  1.3 0.0 copy-start
  1.3 1.6 %copy-done = f32[1024,512]{1,0:T(8,128)S(1)} copy-done((f32[1024,512]{1,0:T(8,128)S(1)}, f32[1024,512]{1,0:T(8,128)}, u32[]{:S(2)}) %copy-start) | copy-done | bytes 2097176
  2.9 0.0 copy-start.1
  2.9 0.8 %copy-done.1 = f32[1024,16]{0,1:T(8,128)S(1)} copy-done((f32[1024,16]{0,1:T(8,128)S(1)}, f32[1024,16]{0,1:T(8,128)}, u32[]{:S(2)}) %copy-start.1) | copy-done | bytes 65560
  3.7 0.0 copy-start.2
  3.7 0.8 %copy-done.2 = f32[1024,16]{0,1:T(8,128)S(1)} copy-done((f32[1024,16]{0,1:T(8,128)S(1)}, f32[1024,16]{0,1:T(8,128)}, u32[]{:S(2)}) %copy-start.2) | copy-done | bytes 65560
  4.5 0.0 copy-start.3
  4.6 0.8 %copy-done.3 = f32[128,128]{1,0:T(8,128)S(1)} copy-done((f32[128,128]{1,0:T(8,128)S(1)}, f32[128,128]{1,0:T(8,128)}, u32[]{:S(2)}) %copy-start.3) | copy-done | bytes 65560
  5.4 29.2 %shard_map.68 = (f32[16,1024]{1,0:T(8,128)S(1)}, f32[16,128]{1,0:T(8,128)S(1)}) custom-call(s32[1]{0:T(128)S(6)} %copy.9.idx_ref, f32[1024,512]{1,0:T(8,128)S(1)} %copy-done, f32[16,1024]{1,0:T(8,128)S(1)} %bitcast.4, f32[16,1024]{1,0:T(8,128)S(1)} %bitcast.5, f32[128,128]{1,0:T(8,128)S(1)} %copy-done.3), custom_call_target="tpu_custom_call" | custom-call | tf_op jit(solution)/shard_map/pallas_call | solution.py:247
  34.6 0.6 %copy.10 = f32[1024,16]{0,1:T(8,128)} copy(f32[1024,16]{0,1:T(8,128)S(1)} %bitcast.6) | data formatting | bytes 131072
  35.2 0.6 %copy.11 = f32[128,16]{0,1:T(8,128)} copy(f32[128,16]{0,1:T(8,128)S(1)} %bitcast.7) | data formatting | bytes 16384
Async XLA Ops:
  1.3 1.6 %copy-start = (f32[1024,512]{1,0:T(8,128)S(1)}, f32[1024,512]{1,0:T(8,128)}, u32[]{:S(2)}) copy-start(f32[1024,512]{1,0:T(8,128)} %trail_ref.1) | copy-start | bytes 6291460
  2.9 0.8 %copy-start.1 = (f32[1024,16]{0,1:T(8,128)S(1)}, f32[1024,16]{0,1:T(8,128)}, u32[]{:S(2)}) copy-start(f32[1024,16]{0,1:T(8,128)} %param.6) | copy-start | bytes 196612
  3.7 0.8 %copy-start.2 = (f32[1024,16]{0,1:T(8,128)S(1)}, f32[1024,16]{0,1:T(8,128)}, u32[]{:S(2)}) copy-start(f32[1024,16]{0,1:T(8,128)} %param.7) | copy-start | bytes 196612
  4.5 0.8 %copy-start.3 = (f32[128,128]{1,0:T(8,128)S(1)}, f32[128,128]{1,0:T(8,128)}, u32[]{:S(2)}) copy-start(f32[128,128]{1,0:T(8,128)} %inv_ref.1) | copy-start | bytes 196612

commit v2 on v1

--- a/solution.py
+++ b/solution.py
@@ -68,6 +68,9 @@
     return (panel_grad, diag_grad)
 
 
+CHUNKS = 2
+
+
 def split(value):
     high = value.astype(jnp.bfloat16)
     return high, (value - high.astype(jnp.float32)).astype(jnp.bfloat16)
@@ -79,17 +82,27 @@
 
 def kernel(
     n_row, n_col, idx_ref, trail_ref, panel_ref, adj_ref, inv_ref, grad_ref, diag_ref,
-    trail_v, t_hi, t_lo, base, z_buf, p_full, stage, cp_buf, q_buf, q_in, d_buf, d_in, d_z,
-    t_sem, z_send, z_recv, p_send, p_recv, c_send, c_recv, q_send, q_recv, d_send, d_recv, dz_send, dz_recv,
+    trail_v, panel_v, adj_v, inv_v, t_hi, t_lo, base, z_buf, p_full, stage, cp_buf, q_buf, sib_in, q_sum, q_in,
+    d_buf, d_in, d_z, loads, z_send, z_recv, p_send, p_recv, f_send, f_recv, c_send, c_recv, s_send, s_recv,
+    q_send, q_recv, d_send, d_recv, dz_send, dz_recv,
 ):
-    thin, rows = panel_ref.shape
-    width = inv_ref.shape[0]
-    cols = trail_ref.shape[1]
+    thin, rows = panel_v.shape
+    width = inv_v.shape[0]
+    cols = trail_v.shape[1]
     ratio = n_col // n_row
+    n_pair = n_col // 2
+    chunks = q_sum.shape[0]
+    part = rows // chunks
     my_row, my_col = lax.axis_index("row"), lax.axis_index("col")
-
-    load = pltpu.make_async_copy(trail_ref, trail_v, t_sem)
-    load.start()
+    my_pair, my_core = my_col // 2, lax.rem(my_col, 2)
+    sibling = {"col": my_pair * 2 + 1 - my_core}
+
+    panel_load = pltpu.make_async_copy(panel_ref, panel_v, loads.at[0])
+    inv_load = pltpu.make_async_copy(inv_ref, inv_v, loads.at[1])
+    adj_load = pltpu.make_async_copy(adj_ref, adj_v, loads.at[2])
+    trail_load = pltpu.make_async_copy(trail_ref, trail_v, loads.at[3])
+    for load in (panel_load, inv_load, adj_load, trail_load):
+        load.start()
 
     def row_at(shift):
         return {"row": lax.rem(my_row + shift, n_row)}
@@ -99,12 +112,19 @@
 
     def col_from(shift):
         return lax.rem(my_col + n_col - shift, n_col)
+
+    def pair_at(shift):
+        return lax.rem(my_pair + shift, n_pair)
+
+    def pair_from(shift):
+        return lax.rem(my_pair + n_pair - shift, n_pair)
 
     barrier = pltpu.get_barrier_semaphore()
     for shift in range(1, n_row):
         pl.semaphore_signal(barrier, inc=1, device_id=row_at(shift), device_id_type=MESH)
     for shift in range(1, n_col):
         pl.semaphore_signal(barrier, inc=1, device_id=col_at(shift), device_id_type=MESH)
+    panel_load.wait()
     pl.semaphore_wait(barrier, n_row + n_col - 2)
 
     def remote(src, dst, send, recv, where):
@@ -112,19 +132,21 @@
             src_ref=src, dst_ref=dst, send_sem=send, recv_sem=recv, device_id=where, device_id_type=MESH
         )
 
-    z_copies = [
-        remote(panel_ref, z_buf.at[s], z_send.at[s], z_recv.at[s], row_at(s)) for s in range(1, n_row)
+    z_copies = [remote(panel_v, z_buf.at[s], z_send.at[s], z_recv.at[s], row_at(s)) for s in range(1, n_row)]
+    p_copies = [remote(panel_v, p_full.at[my_col], p_send.at[0], p_recv.at[0], sibling)]
+    p_copies += [
+        remote(
+            panel_v, p_full.at[my_col], p_send.at[s], p_recv.at[s], {"col": pair_at(s) * 2 + my_core}
+        )
+        for s in range(1, n_pair)
     ]
-    for copy in z_copies:
+    for copy in z_copies + p_copies:
         copy.start()
-    p_copies = [
-        remote(panel_ref, p_full.at[my_col], p_send.at[s], p_recv.at[s], col_at(s)) for s in range(1, n_col)
-    ]
 
     index_k = idx_ref[0]
 
     def forward(shift):
-        piece = panel_ref[...] if shift == 0 else z_buf[shift]
+        piece = panel_v[...] if shift == 0 else z_buf[shift]
         source = lax.rem(my_row + n_row - shift, n_row)
         for group in range(ratio):
             target = source + n_row * group
@@ -132,12 +154,12 @@
             slot = shift * ratio + group
             for block in range(rows // (width * ratio)):
                 at = block * ratio * width
-                part = piece[:, at : at + width]
+                chosen = piece[:, at : at + width]
                 for other in range(1, ratio):
-                    part = jnp.where(
-                        offset == other, piece[:, at + other * width : at + (other + 1) * width], part
+                    chosen = jnp.where(
+                        offset == other, piece[:, at + other * width : at + (other + 1) * width], chosen
                     )
-                stage[slot, :, block * width : (block + 1) * width] = part
+                stage[slot, :, block * width : (block + 1) * width] = chosen
             away = lax.rem(target + n_col - my_col, n_col)
 
             @pl.when(away != 0)
@@ -151,26 +173,32 @@
                 cp_buf[my_col] = stage[slot]
 
     forward(0)
-    for copy in p_copies:
-        copy.start()
-    p_full[my_col] = panel_ref[...]
-
-    adj_hi, adj_lo = split(adj_ref[...])
-    inv_hi, inv_lo = split(inv_ref[pl.ds(pl.multiple_of(my_col * thin, 8), thin), :])
-    base[...] = dot(
-        jnp.concatenate([inv_hi, inv_lo, inv_hi], 0), jnp.concatenate([adj_hi, adj_hi, adj_lo], 0), ((0,), (0,))
-    )
-    load.wait()
-    trail_t = trail_v[...].T
-    hi, lo = split(trail_t)
+    p_full[my_col] = panel_v[...]
+
+    trail_load.wait()
+    hi, lo = split(trail_v[...].T)
     t_hi[...] = hi
     t_lo[...] = lo
 
+    relays = []
     for shift in range(1, n_row):
         z_copies[shift - 1].wait_recv()
         forward(shift)
-
-    inv_hi, inv_lo = split(inv_ref[...].T)
+    for s in range(1, n_pair):
+        slot = p_full.at[pair_from(s) * 2 + my_core]
+        remote(slot, slot, p_send.at[s], p_recv.at[s], sibling).wait_recv()
+        relay = remote(slot, slot, f_send.at[s], f_recv.at[s], sibling)
+        relay.start()
+        relays.append(relay)
+
+    adj_load.wait()
+    inv_load.wait()
+    adj_hi, adj_lo = split(adj_v[...])
+    inv_hi, inv_lo = split(inv_v[pl.ds(pl.multiple_of(my_col * thin, 8), thin), :])
+    base[...] = dot(
+        jnp.concatenate([inv_hi, inv_lo, inv_hi], 0), jnp.concatenate([adj_hi, adj_hi, adj_lo], 0), ((0,), (0,))
+    )
+    inv_hi, inv_lo = split(inv_v[...].T)
     for s in range(1, n_col):
         where = cp_buf.at[col_from(s)]
         remote(where, where, c_send.at[s], c_recv.at[s], col_at(s)).wait_recv()
@@ -179,24 +207,47 @@
         jnp.concatenate([inv_hi, inv_lo, inv_hi], 1), jnp.concatenate([cp_hi, cp_hi, cp_lo], 0), ((1,), (0,))
     )
     w_hi, w_lo = split(w)
-    both = dot(jnp.concatenate([w_hi, w_lo], 0), t_hi[...], ((1,), (0,)))
-    q = base[...] + both[:width] + both[width:] + dot(w_hi, t_lo[...], ((1,), (0,)))
-    q_buf[...] = q.reshape(n_col, thin, rows)
+    w_both = jnp.concatenate([w_hi, w_lo], 0)
+
+    q_parts, s_copies = [], []
+    for h in range(chunks):
+        at = slice(h * part, (h + 1) * part)
+        both = dot(w_both, t_hi[:, at], ((1,), (0,)))
+        q = base[:, at] + both[:width] + both[width:] + dot(w_hi, t_lo[:, at], ((1,), (0,)))
+        q_parts.append(q)
+        by_core = q.reshape(n_pair, 2, thin, part)
+        for core in range(2):
+            q_buf[h, core] = by_core[:, core]
+        copy = remote(q_buf.at[h, 1 - my_core], sib_in.at[h], s_send.at[h], s_recv.at[h], sibling)
+        copy.start()
+        s_copies.append(copy)
+
     q_copies = []
-    for s in range(1, n_col):
-        copy = remote(
-            q_buf.at[lax.rem(my_col + s, n_col)], q_in.at[s], q_send.at[s], q_recv.at[s], col_at(s)
-        )
-        copy.start()
-        q_copies.append(copy)
-
-    for s in range(1, n_col):
-        where = p_full.at[col_from(s)]
-        remote(where, where, p_send.at[s], p_recv.at[s], col_at(s)).wait_recv()
-    q_hi, q_lo = split(q)
-    f_hi, f_lo = split(p_full[...].reshape(width, rows))
+
+    def reduce_out(h):
+        s_copies[h].wait_recv()
+        q_sum[h] = q_buf[h, my_core] + sib_in[h]
+        for s in range(1, n_pair):
+            sem = h * n_pair + s
+            copy = remote(
+                q_sum.at[h, pair_at(s)], q_in.at[h, s], q_send.at[sem], q_recv.at[sem],
+                {"col": pair_at(s) * 2 + my_core},
+            )
+            copy.start()
+            q_copies.append(copy)
+
+    reduce_out(0)
+
+    p_copies[0].wait_recv()
+    for s in range(1, n_pair):
+        slot = p_full.at[pair_from(s) * 2 + 1 - my_core]
+        remote(slot, slot, f_send.at[s], f_recv.at[s], sibling).wait_recv()
+    d = jnp.zeros((width, width), jnp.float32)
     nt = ((1,), (1,))
-    d = -(dot(f_hi, q_hi, nt) + dot(f_hi, q_lo, nt) + dot(f_lo, q_hi, nt))
+    for h in range(chunks):
+        q_hi, q_lo = split(q_parts[h])
+        f_hi, f_lo = split(p_full[:, :, h * part : (h + 1) * part].reshape(width, part))
+        d = d - (dot(f_hi, q_hi, nt) + dot(f_hi, q_lo, nt) + dot(f_lo, q_hi, nt))
     d_buf[...] = d.reshape(n_col, thin, width)
     d_copies = []
     for s in range(1, n_col):
@@ -205,6 +256,9 @@
         )
         copy.start()
         d_copies.append(copy)
+    for h in range(1, chunks):
+        reduce_out(h)
+
     total = d_buf[my_col]
     for s in range(1, n_col):
         d_copies[s - 1].wait_recv()
@@ -216,11 +270,12 @@
         copy.start()
         dz_copies.append(copy)
 
-    total = q_buf[my_col]
-    for s in range(1, n_col):
-        q_copies[s - 1].wait_recv()
-        total = total + q_in[s]
-    grad_ref[...] = total
+    for h in range(chunks):
+        total = q_sum[h, my_pair]
+        for s in range(1, n_pair):
+            q_copies[h * (n_pair - 1) + s - 1].wait_recv()
+            total = total + q_in[h, s]
+        grad_ref[:, h * part : (h + 1) * part] = total
 
     for s in range(1, n_row):
         where = d_z.at[lax.rem(my_row + n_row - s, n_row)]
@@ -232,7 +287,7 @@
 
     for s in range(1, n_col):
         remote(stage.at[0], cp_buf.at[my_col], c_send.at[s], c_recv.at[s], col_at(s)).wait_send()
-    for copy in z_copies + p_copies + q_copies + d_copies + dz_copies:
+    for copy in z_copies + p_copies + relays + s_copies + q_copies + d_copies + dz_copies:
         copy.wait_send()
 
 
@@ -241,16 +296,21 @@
     cols = trail_adjoint.shape[1]
     width = inv_diag.shape[0]
     n_row, n_col = lax.axis_size("row"), lax.axis_size("col")
+    n_pair, chunks = n_col // 2, CHUNKS
+    part = rows // chunks
     f32, bf16 = jnp.float32, jnp.bfloat16
-    vmem = pl.BlockSpec(memory_space=pltpu.VMEM)
+    vmem, hbm = pl.BlockSpec(memory_space=pltpu.VMEM), pl.BlockSpec(memory_space=pl.ANY)
     dma = pltpu.SemaphoreType.DMA
     grad, diag = pl.pallas_call(
         functools.partial(kernel, n_row, n_col),
         out_shape=(jax.ShapeDtypeStruct((thin, rows), f32), jax.ShapeDtypeStruct((thin, width), f32)),
-        in_specs=[pl.BlockSpec(memory_space=pltpu.SMEM), pl.BlockSpec(memory_space=pl.ANY), vmem, vmem, vmem],
+        in_specs=[pl.BlockSpec(memory_space=pltpu.SMEM), hbm, hbm, hbm, hbm],
         out_specs=(vmem, vmem),
         scratch_shapes=[
             pltpu.VMEM((rows, cols), f32),
+            pltpu.VMEM((thin, rows), f32),
+            pltpu.VMEM((thin, rows), f32),
+            pltpu.VMEM((width, width), f32),
             pltpu.VMEM((cols, rows), bf16),
             pltpu.VMEM((cols, rows), bf16),
             pltpu.VMEM((width, rows), f32),
@@ -258,21 +318,25 @@
             pltpu.VMEM((n_col, thin, rows), f32),
             pltpu.VMEM((n_col, thin, cols), f32),
             pltpu.VMEM((n_col, thin, cols), f32),
-            pltpu.VMEM((n_col, thin, rows), f32),
-            pltpu.VMEM((n_col, thin, rows), f32),
+            pltpu.VMEM((chunks, 2, n_pair, thin, part), f32),
+            pltpu.VMEM((chunks, n_pair, thin, part), f32),
+            pltpu.VMEM((chunks, n_pair, thin, part), f32),
+            pltpu.VMEM((chunks, n_pair, thin, part), f32),
             pltpu.VMEM((n_col, thin, width), f32),
             pltpu.VMEM((n_col, thin, width), f32),
             pltpu.VMEM((n_row, thin, width), f32),
-            dma,
+            dma((4,)),
             dma((n_row,)), dma((n_row,)),
+            dma((n_pair,)), dma((n_pair,)),
+            dma((n_pair,)), dma((n_pair,)),
             dma((n_col,)), dma((n_col,)),
-            dma((n_col,)), dma((n_col,)),
-            dma((n_col,)), dma((n_col,)),
+            dma((chunks,)), dma((chunks,)),
+            dma((chunks * n_pair,)), dma((chunks * n_pair,)),
             dma((n_col,)), dma((n_col,)),
             dma((n_row,)), dma((n_row,)),
         ],
         compiler_params=pltpu.CompilerParams(
-            collective_id=0, has_side_effects=True, vmem_limit_bytes=40 * 2**20
+            collective_id=0, has_side_effects=True, vmem_limit_bytes=60 * 2**20
         ),
     )(panel_index, trail_adjoint, panel.T, panel_adjoint.T, inv_diag)
     return grad.T, diag.T

time: 36.2 us -> 31 us (0.86)
  local copies, waits for them, and re-layouts: 5.33 us -> 2.77 us
  Pallas kernels: 29.2 us -> 26.7 us
    unnamed x10 -> x2, local copies, waits for them, and re-layouts: 5.33 us -> 2.77 us
    pallas_call x1, Pallas kernels: 29.2 us -> 26.7 us  [fused(): pl.pallas_call(functools.partial(kernel, n_row, n_col), out_shape=(jax.Sh...]
where the time goes in v2:
time: 31 us; the launch traced here: 30.8 us
  Pallas kernels  26.7 us (86%)
  local copies, waits for them, and re-layouts  2.77 us (9%)
  between operations  1.29 us (4%)
    pallas_call x1, Pallas kernels, fused(): pl.pallas_call(functools.partial(kernel, n_row, n_col), out_shape=(jax.Sh...  26.7 us
    unnamed x2, local copies, waits for them, and re-layouts  2.77 us

profile of v2, /device:TPU:0, one launch (start us, length us, event | category | flops | bytes accessed | tf_op | source)
XLA Modules:
  0.0 30.8 jit_solution(1748336880384423825)
XLA Ops:
  1.3 26.7 %shard_map.68 = (f32[16,1024]{1,0:T(8,128)}, f32[16,128]{1,0:T(8,128)}) custom-call(s32[1]{0:T(128)S(6)} %copy.9.idx_ref, f32[1024,512]{1,0:T(8,128)} %trail_ref.1, f32[16,1024]{1,0:T(8,128)} %bitcast.4, f32[16,1024]{1,0:T(8,128)} %bitcast.5, f32[128,128]{1,0:T(8,128)} %inv_ref.1), custom_call_target="tpu_custom_call" | custom-call | tf_op jit(solution)/shard_map/pallas_call | solution.py:304
  28.0 1.5 %copy.10 = f32[1024,16]{0,1:T(8,128)} copy(f32[1024,16]{0,1:T(8,128)} %bitcast.6) | data formatting | bytes 131072
  29.5 1.3 %copy.11 = f32[128,16]{0,1:T(8,128)} copy(f32[128,16]{0,1:T(8,128)} %bitcast.7) | data formatting | bytes 16384

commit v3 on v2

--- a/solution.py
+++ b/solution.py
@@ -69,6 +69,7 @@
 
 
 CHUNKS = 2
+HALVES = 2
 
 
 def split(value):
@@ -93,6 +94,8 @@
     n_pair = n_col // 2
     chunks = q_sum.shape[0]
     part = rows // chunks
+    halves = cp_buf.shape[0]
+    half_rows, half_cols = rows // halves, cols // halves
     my_row, my_col = lax.axis_index("row"), lax.axis_index("col")
     my_pair, my_core = my_col // 2, lax.rem(my_col, 2)
     sibling = {"col": my_pair * 2 + 1 - my_core}
@@ -113,11 +116,8 @@
     def col_from(shift):
         return lax.rem(my_col + n_col - shift, n_col)
 
-    def pair_at(shift):
-        return lax.rem(my_pair + shift, n_pair)
-
-    def pair_from(shift):
-        return lax.rem(my_pair + n_pair - shift, n_pair)
+    def pair_at(mask):
+        return my_pair ^ mask
 
     barrier = pltpu.get_barrier_semaphore()
     for shift in range(1, n_row):
@@ -132,7 +132,13 @@
             src_ref=src, dst_ref=dst, send_sem=send, recv_sem=recv, device_id=where, device_id_type=MESH
         )
 
-    z_copies = [remote(panel_v, z_buf.at[s], z_send.at[s], z_recv.at[s], row_at(s)) for s in range(1, n_row)]
+    def z_copy(s, h):
+        lanes, sem = pl.ds(h * half_rows, half_rows), s * halves + h
+        return remote(
+            panel_v.at[:, lanes], z_buf.at[s, :, lanes], z_send.at[sem], z_recv.at[sem], row_at(s)
+        )
+
+    z_copies = [z_copy(s, h) for h in range(halves) for s in range(1, n_row)]
     p_copies = [remote(panel_v, p_full.at[my_col], p_send.at[0], p_recv.at[0], sibling)]
     p_copies += [
         remote(
@@ -145,34 +151,37 @@
 
     index_k = idx_ref[0]
 
-    def forward(shift):
-        piece = panel_v[...] if shift == 0 else z_buf[shift]
+    def forward(shift, h):
+        lanes = slice(h * half_rows, (h + 1) * half_rows)
+        piece = panel_v[:, lanes] if shift == 0 else z_buf[shift, :, lanes]
         source = lax.rem(my_row + n_row - shift, n_row)
         for group in range(ratio):
             target = source + n_row * group
             offset = jnp.mod(target - index_k - 1, n_col) // n_row
             slot = shift * ratio + group
-            for block in range(rows // (width * ratio)):
+            for block in range(half_rows // (width * ratio)):
                 at = block * ratio * width
                 chosen = piece[:, at : at + width]
                 for other in range(1, ratio):
                     chosen = jnp.where(
                         offset == other, piece[:, at + other * width : at + (other + 1) * width], chosen
                     )
-                stage[slot, :, block * width : (block + 1) * width] = chosen
+                stage[h, slot, :, block * width : (block + 1) * width] = chosen
             away = lax.rem(target + n_col - my_col, n_col)
 
             @pl.when(away != 0)
             def _():
+                sem = h * n_col + away
                 remote(
-                    stage.at[slot], cp_buf.at[my_col], c_send.at[away], c_recv.at[away], {"col": target}
+                    stage.at[h, slot], cp_buf.at[h, my_col], c_send.at[sem], c_recv.at[sem], {"col": target}
                 ).start()
 
             @pl.when(away == 0)
             def _():
-                cp_buf[my_col] = stage[slot]
-
-    forward(0)
+                cp_buf[h, my_col] = stage[h, slot]
+
+    for h in range(halves):
+        forward(0, h)
     p_full[my_col] = panel_v[...]
 
     trail_load.wait()
@@ -181,11 +190,8 @@
     t_lo[...] = lo
 
     relays = []
-    for shift in range(1, n_row):
-        z_copies[shift - 1].wait_recv()
-        forward(shift)
     for s in range(1, n_pair):
-        slot = p_full.at[pair_from(s) * 2 + my_core]
+        slot = p_full.at[pair_at(s) * 2 + my_core]
         remote(slot, slot, p_send.at[s], p_recv.at[s], sibling).wait_recv()
         relay = remote(slot, slot, f_send.at[s], f_recv.at[s], sibling)
         relay.start()
@@ -199,35 +205,83 @@
         jnp.concatenate([inv_hi, inv_lo, inv_hi], 0), jnp.concatenate([adj_hi, adj_hi, adj_lo], 0), ((0,), (0,))
     )
     inv_hi, inv_lo = split(inv_v[...].T)
-    for s in range(1, n_col):
-        where = cp_buf.at[col_from(s)]
-        remote(where, where, c_send.at[s], c_recv.at[s], col_at(s)).wait_recv()
-    cp_hi, cp_lo = split(cp_buf[...].reshape(width, cols))
-    w = -2.0 * dot(
-        jnp.concatenate([inv_hi, inv_lo, inv_hi], 1), jnp.concatenate([cp_hi, cp_hi, cp_lo], 0), ((1,), (0,))
-    )
-    w_hi, w_lo = split(w)
-    w_both = jnp.concatenate([w_hi, w_lo], 0)
-
-    q_parts, s_copies = [], []
+    inv_all = jnp.concatenate([inv_hi, inv_lo, inv_hi], 1)
+
+    def forward_all(h):
+        for shift in range(1, n_row):
+            z_copies[h * (n_row - 1) + shift - 1].wait_recv()
+            forward(shift, h)
+
+    for h in range(halves - 1):
+        forward_all(h)
+
+    p_copies[0].wait_recv()
+    for s in range(1, n_pair):
+        slot = p_full.at[pair_at(s) * 2 + 1 - my_core]
+        remote(slot, slot, f_send.at[s], f_recv.at[s], sibling).wait_recv()
+    nt, nn = ((1,), (1,)), ((1,), (0,))
+    f_hi, f_lo = split(p_full[...].reshape(width, rows))
+    t_high, t_low = split(trail_v[...])
+    x = dot(jnp.concatenate([f_hi, f_lo], 0), t_high, nn)
+    x = x[:width] + x[width:] + dot(f_hi, t_low, nn)
+    x_hi, x_lo = split(x)
+    b_hi, b_lo = split(base[...])
+    d = dot(f_hi, b_hi, nt) + dot(f_hi, b_lo, nt) + dot(f_lo, b_hi, nt)
+
+    forward_all(halves - 1)
+
+    def weights(h):
+        for s in range(1, n_col):
+            where, sem = cp_buf.at[h, col_from(s)], h * n_col + s
+            remote(where, where, c_send.at[sem], c_recv.at[sem], col_at(s)).wait_recv()
+        cp_hi, cp_lo = split(cp_buf[h].reshape(width, half_cols))
+        w = -2.0 * dot(inv_all, jnp.concatenate([cp_hi, cp_hi, cp_lo], 0), nn)
+        return split(w)
+
+    def term(w_hi, w_lo, h, at):
+        deep = slice(h * half_cols, (h + 1) * half_cols)
+        both = dot(jnp.concatenate([w_hi, w_lo], 0), t_hi[deep, at], nn)
+        return both[:width] + both[width:] + dot(w_hi, t_lo[deep, at], nn)
+
+    def diag_term(w_hi, w_lo, h):
+        deep = slice(h * half_cols, (h + 1) * half_cols)
+        x_h, x_l = x_hi[:, deep], x_lo[:, deep]
+        return dot(x_h, w_hi, nt) + dot(x_h, w_lo, nt) + dot(x_l, w_hi, nt)
+
+    for half in range(halves - 1):
+        w_hi, w_lo = weights(half)
+        for h in range(chunks):
+            at = slice(h * part, (h + 1) * part)
+            base[:, at] += term(w_hi, w_lo, half, at)
+        d = d + diag_term(w_hi, w_lo, half)
+    w_hi, w_lo = weights(halves - 1)
+
+    s_copies, d_copies = [], []
     for h in range(chunks):
         at = slice(h * part, (h + 1) * part)
-        both = dot(w_both, t_hi[:, at], ((1,), (0,)))
-        q = base[:, at] + both[:width] + both[width:] + dot(w_hi, t_lo[:, at], ((1,), (0,)))
-        q_parts.append(q)
+        q = base[:, at] + term(w_hi, w_lo, halves - 1, at)
         by_core = q.reshape(n_pair, 2, thin, part)
         for core in range(2):
             q_buf[h, core] = by_core[:, core]
         copy = remote(q_buf.at[h, 1 - my_core], sib_in.at[h], s_send.at[h], s_recv.at[h], sibling)
         copy.start()
         s_copies.append(copy)
+        if h == 0:
+            d = -(d + diag_term(w_hi, w_lo, halves - 1))
+            d_buf[...] = d.reshape(n_col, thin, width)
+            for s in range(1, n_col):
+                copy = remote(
+                    d_buf.at[lax.rem(my_col + s, n_col)], d_in.at[s], d_send.at[s], d_recv.at[s], col_at(s)
+                )
+                copy.start()
+                d_copies.append(copy)
 
     q_copies = []
 
     def reduce_out(h):
         s_copies[h].wait_recv()
         q_sum[h] = q_buf[h, my_core] + sib_in[h]
-        for s in range(1, n_pair):
+        for s in range(n_pair - 1, 0, -1):
             sem = h * n_pair + s
             copy = remote(
                 q_sum.at[h, pair_at(s)], q_in.at[h, s], q_send.at[sem], q_recv.at[sem],
@@ -236,27 +290,7 @@
             copy.start()
             q_copies.append(copy)
 
-    reduce_out(0)
-
-    p_copies[0].wait_recv()
-    for s in range(1, n_pair):
-        slot = p_full.at[pair_from(s) * 2 + 1 - my_core]
-        remote(slot, slot, f_send.at[s], f_recv.at[s], sibling).wait_recv()
-    d = jnp.zeros((width, width), jnp.float32)
-    nt = ((1,), (1,))
     for h in range(chunks):
-        q_hi, q_lo = split(q_parts[h])
-        f_hi, f_lo = split(p_full[:, :, h * part : (h + 1) * part].reshape(width, part))
-        d = d - (dot(f_hi, q_hi, nt) + dot(f_hi, q_lo, nt) + dot(f_lo, q_hi, nt))
-    d_buf[...] = d.reshape(n_col, thin, width)
-    d_copies = []
-    for s in range(1, n_col):
-        copy = remote(
-            d_buf.at[lax.rem(my_col + s, n_col)], d_in.at[s], d_send.at[s], d_recv.at[s], col_at(s)
-        )
-        copy.start()
-        d_copies.append(copy)
-    for h in range(1, chunks):
         reduce_out(h)
 
     total = d_buf[my_col]
@@ -272,8 +306,8 @@
 
     for h in range(chunks):
         total = q_sum[h, my_pair]
-        for s in range(1, n_pair):
-            q_copies[h * (n_pair - 1) + s - 1].wait_recv()
+        for s in range(n_pair - 1, 0, -1):
+            q_copies[h * (n_pair - 1) + n_pair - 1 - s].wait_recv()
             total = total + q_in[h, s]
         grad_ref[:, h * part : (h + 1) * part] = total
 
@@ -285,8 +319,12 @@
         total = total + d_z[r]
     diag_ref[...] = total
 
-    for s in range(1, n_col):
-        remote(stage.at[0], cp_buf.at[my_col], c_send.at[s], c_recv.at[s], col_at(s)).wait_send()
+    for h in range(halves):
+        for s in range(1, n_col):
+            sem = h * n_col + s
+            remote(
+                stage.at[h, 0], cp_buf.at[h, my_col], c_send.at[sem], c_recv.at[sem], col_at(s)
+            ).wait_send()
     for copy in z_copies + p_copies + relays + s_copies + q_copies + d_copies + dz_copies:
         copy.wait_send()
 
@@ -296,14 +334,14 @@
     cols = trail_adjoint.shape[1]
     width = inv_diag.shape[0]
     n_row, n_col = lax.axis_size("row"), lax.axis_size("col")
-    n_pair, chunks = n_col // 2, CHUNKS
+    n_pair, chunks, halves = n_col // 2, CHUNKS, HALVES
     part = rows // chunks
     f32, bf16 = jnp.float32, jnp.bfloat16
     vmem, hbm = pl.BlockSpec(memory_space=pltpu.VMEM), pl.BlockSpec(memory_space=pl.ANY)
     dma = pltpu.SemaphoreType.DMA
     grad, diag = pl.pallas_call(
         functools.partial(kernel, n_row, n_col),
-        out_shape=(jax.ShapeDtypeStruct((thin, rows), f32), jax.ShapeDtypeStruct((thin, width), f32)),
+        out_shape=(pltpu.VMEM((thin, rows), f32), pltpu.VMEM((thin, width), f32)),
         in_specs=[pl.BlockSpec(memory_space=pltpu.SMEM), hbm, hbm, hbm, hbm],
         out_specs=(vmem, vmem),
         scratch_shapes=[
@@ -316,8 +354,8 @@
             pltpu.VMEM((width, rows), f32),
             pltpu.VMEM((n_row, thin, rows), f32),
             pltpu.VMEM((n_col, thin, rows), f32),
-            pltpu.VMEM((n_col, thin, cols), f32),
-            pltpu.VMEM((n_col, thin, cols), f32),
+            pltpu.VMEM((halves, n_col, thin, cols // halves), f32),
+            pltpu.VMEM((halves, n_col, thin, cols // halves), f32),
             pltpu.VMEM((chunks, 2, n_pair, thin, part), f32),
             pltpu.VMEM((chunks, n_pair, thin, part), f32),
             pltpu.VMEM((chunks, n_pair, thin, part), f32),
@@ -326,10 +364,10 @@
             pltpu.VMEM((n_col, thin, width), f32),
             pltpu.VMEM((n_row, thin, width), f32),
             dma((4,)),
-            dma((n_row,)), dma((n_row,)),
+            dma((n_row * halves,)), dma((n_row * halves,)),
             dma((n_pair,)), dma((n_pair,)),
             dma((n_pair,)), dma((n_pair,)),
-            dma((n_col,)), dma((n_col,)),
+            dma((n_col * halves,)), dma((n_col * halves,)),
             dma((chunks,)), dma((chunks,)),
             dma((chunks * n_pair,)), dma((chunks * n_pair,)),
             dma((n_col,)), dma((n_col,)),

time: 31 us -> 28 us (0.903)
  local copies, waits for them, and re-layouts: 2.77 us -> 1.23 us
  Pallas kernels: 26.7 us -> 25.4 us
    unnamed x2, local copies, waits for them, and re-layouts: 2.77 us -> 1.23 us
    pallas_call x1, Pallas kernels: 26.7 us -> 25.4 us  [fused(): pl.pallas_call(functools.partial(kernel, n_row, n_col), out_shape=(pltpu....]
where the time goes in v3:
time: 28 us; the launch traced here: 27.9 us
  Pallas kernels  25.4 us (91%)
  between operations  1.29 us (5%)
  local copies, waits for them, and re-layouts  1.23 us (4%)
    pallas_call x1, Pallas kernels, fused(): pl.pallas_call(functools.partial(kernel, n_row, n_col), out_shape=(pltpu....  25.4 us
    unnamed x2, local copies, waits for them, and re-layouts  1.23 us

profile of v3, /device:TPU:0, one launch (start us, length us, event | category | flops | bytes accessed | tf_op | source)
XLA Modules:
  0.0 27.9 jit_solution(5501088173882806856)
XLA Ops:
  1.3 25.4 %shard_map.68 = (f32[16,1024]{1,0:T(8,128)S(1)}, f32[16,128]{1,0:T(8,128)S(1)}) custom-call(s32[1]{0:T(128)S(6)} %copy.11.idx_ref, f32[1024,512]{1,0:T(8,128)} %trail_ref.1, f32[16,1024]{1,0:T(8,128)} %bitcast.6, f32[16,1024]{1,0:T(8,128)} %bitcast.7, f32[128,128]{1,0:T(8,128)} %inv_ref.1), custom_call_target="tpu_custom_call" | custom-call | tf_op jit(solution)/shard_map/pallas_call | solution.py:342
  26.7 0.6 %copy.9 = f32[1024,16]{0,1:T(8,128)} copy(f32[1024,16]{0,1:T(8,128)S(1)} %bitcast.4) | data formatting | bytes 131072
  27.3 0.6 %copy.10 = f32[128,16]{0,1:T(8,128)} copy(f32[128,16]{0,1:T(8,128)S(1)} %bitcast.5) | data formatting | bytes 16384

commit v4 on v3

--- a/solution.py
+++ b/solution.py
@@ -132,13 +132,31 @@
             src_ref=src, dst_ref=dst, send_sem=send, recv_sem=recv, device_id=where, device_id_type=MESH
         )
 
-    def z_copy(s, h):
-        lanes, sem = pl.ds(h * half_rows, half_rows), s * halves + h
-        return remote(
-            panel_v.at[:, lanes], z_buf.at[s, :, lanes], z_send.at[sem], z_recv.at[sem], row_at(s)
-        )
-
-    z_copies = [z_copy(s, h) for h in range(halves) for s in range(1, n_row)]
+    def z_copy(source, h, step):
+        lanes, sem = pl.ds(h * half_rows, half_rows), source * halves + h
+        sends = z_send.at[(step + 1) // 2 * n_row * halves + sem]
+        slot = z_buf.at[source, :, lanes]
+        return remote(slot, slot, sends, z_recv.at[sem], {"row": jnp.clip(my_row + step, 0, n_row - 1)})
+
+    def has_next(step):
+        return my_row < n_row - 1 if step > 0 else my_row > 0
+
+    def pass_on(source, h, step, do):
+        @pl.when(has_next(step))
+        def _():
+            do(z_copy(source, h, step))
+
+    def from_behind(distance, step, do):
+        source = my_row - distance * step
+
+        @pl.when(source >= 0 if step > 0 else source < n_row)
+        def _():
+            do(source)
+
+    z_buf[my_row] = panel_v[...]
+    for h in range(halves):
+        for step in (1, -1):
+            pass_on(my_row, h, step, lambda copy: copy.start())
     p_copies = [remote(panel_v, p_full.at[my_col], p_send.at[0], p_recv.at[0], sibling)]
     p_copies += [
         remote(
@@ -146,19 +164,18 @@
         )
         for s in range(1, n_pair)
     ]
-    for copy in z_copies + p_copies:
+    for copy in p_copies:
         copy.start()
 
     index_k = idx_ref[0]
 
-    def forward(shift, h):
+    def forward(source, h):
         lanes = slice(h * half_rows, (h + 1) * half_rows)
-        piece = panel_v[:, lanes] if shift == 0 else z_buf[shift, :, lanes]
-        source = lax.rem(my_row + n_row - shift, n_row)
+        piece = z_buf[source, :, lanes]
         for group in range(ratio):
             target = source + n_row * group
             offset = jnp.mod(target - index_k - 1, n_col) // n_row
-            slot = shift * ratio + group
+            slot = source * ratio + group
             for block in range(half_rows // (width * ratio)):
                 at = block * ratio * width
                 chosen = piece[:, at : at + width]
@@ -181,7 +198,7 @@
                 cp_buf[h, my_col] = stage[h, slot]
 
     for h in range(halves):
-        forward(0, h)
+        forward(my_row, h)
     p_full[my_col] = panel_v[...]
 
     trail_load.wait()
@@ -189,6 +206,18 @@
     t_hi[...] = hi
     t_lo[...] = lo
 
+    def hop(distance):
+        for h in range(halves):
+            for step in (1, -1):
+
+                def receive(source, h=h, step=step):
+                    z_copy(source, h, step).wait_recv()
+                    pass_on(source, h, step, lambda copy: copy.start())
+                    forward(source, h)
+
+                from_behind(distance, step, receive)
+
+    hop(1)
     relays = []
     for s in range(1, n_pair):
         slot = p_full.at[pair_at(s) * 2 + my_core]
@@ -207,13 +236,7 @@
     inv_hi, inv_lo = split(inv_v[...].T)
     inv_all = jnp.concatenate([inv_hi, inv_lo, inv_hi], 1)
 
-    def forward_all(h):
-        for shift in range(1, n_row):
-            z_copies[h * (n_row - 1) + shift - 1].wait_recv()
-            forward(shift, h)
-
-    for h in range(halves - 1):
-        forward_all(h)
+    hop(2)
 
     p_copies[0].wait_recv()
     for s in range(1, n_pair):
@@ -228,7 +251,8 @@
     b_hi, b_lo = split(base[...])
     d = dot(f_hi, b_hi, nt) + dot(f_hi, b_lo, nt) + dot(f_lo, b_hi, nt)
 
-    forward_all(halves - 1)
+    for distance in range(3, n_row):
+        hop(distance)
 
     def weights(h):
         for s in range(1, n_col):
@@ -325,7 +349,13 @@
             remote(
                 stage.at[h, 0], cp_buf.at[h, my_col], c_send.at[sem], c_recv.at[sem], col_at(s)
             ).wait_send()
-    for copy in z_copies + p_copies + relays + s_copies + q_copies + d_copies + dz_copies:
+    for h in range(halves):
+        for step in (1, -1):
+            for distance in range(n_row):
+                from_behind(
+                    distance, step, lambda source: pass_on(source, h, step, lambda copy: copy.wait_send())
+                )
+    for copy in p_copies + relays + s_copies + q_copies + d_copies + dz_copies:
         copy.wait_send()
 
 
@@ -364,7 +394,7 @@
             pltpu.VMEM((n_col, thin, width), f32),
             pltpu.VMEM((n_row, thin, width), f32),
             dma((4,)),
-            dma((n_row * halves,)), dma((n_row * halves,)),
+            dma((2 * n_row * halves,)), dma((n_row * halves,)),
             dma((n_pair,)), dma((n_pair,)),
             dma((n_pair,)), dma((n_pair,)),
             dma((n_col * halves,)), dma((n_col * halves,)),

time: 28 us -> 29.3 us (1.046)
  Pallas kernels: 25.4 us -> 26.6 us
    pallas_call x1, Pallas kernels: 25.4 us -> 26.6 us  [fused(): pl.pallas_call(functools.partial(kernel, n_row, n_col), out_shape=(pltpu....]
where the time goes in v4:
time: 29.3 us; the launch traced here: 29.1 us
  Pallas kernels  26.6 us (91%)
  between operations  1.29 us (4%)
  local copies, waits for them, and re-layouts  1.23 us (4%)
    pallas_call x1, Pallas kernels, fused(): pl.pallas_call(functools.partial(kernel, n_row, n_col), out_shape=(pltpu....  26.6 us
    unnamed x2, local copies, waits for them, and re-layouts  1.23 us

profile of v4, /device:TPU:0, one launch (start us, length us, event | category | flops | bytes accessed | tf_op | source)
XLA Modules:
  0.0 29.1 jit_solution(10770378362882540345)
XLA Ops:
  1.3 26.6 %shard_map.68 = (f32[16,1024]{1,0:T(8,128)S(1)}, f32[16,128]{1,0:T(8,128)S(1)}) custom-call(s32[1]{0:T(128)S(6)} %copy.11.idx_ref, f32[1024,512]{1,0:T(8,128)} %trail_ref.1, f32[16,1024]{1,0:T(8,128)} %bitcast.6, f32[16,1024]{1,0:T(8,128)} %bitcast.7, f32[128,128]{1,0:T(8,128)} %inv_ref.1), custom_call_target="tpu_custom_call" | custom-call | tf_op jit(solution)/shard_map/pallas_call | solution.py:372
  27.9 0.6 %copy.9 = f32[1024,16]{0,1:T(8,128)} copy(f32[1024,16]{0,1:T(8,128)S(1)} %bitcast.4) | data formatting | bytes 131072
  28.5 0.6 %copy.10 = f32[128,16]{0,1:T(8,128)} copy(f32[128,16]{0,1:T(8,128)S(1)} %bitcast.5) | data formatting | bytes 16384

commit v5 on v2

--- a/solution.py
+++ b/solution.py
@@ -176,14 +176,11 @@
     p_full[my_col] = panel_v[...]
 
     trail_load.wait()
-    hi, lo = split(trail_v[...].T)
-    t_hi[...] = hi
-    t_lo[...] = lo
+    t_high, t_low = split(trail_v[...])
+    t_hi[...] = t_high
+    t_lo[...] = t_low
 
     relays = []
-    for shift in range(1, n_row):
-        z_copies[shift - 1].wait_recv()
-        forward(shift)
     for s in range(1, n_pair):
         slot = p_full.at[pair_from(s) * 2 + my_core]
         remote(slot, slot, p_send.at[s], p_recv.at[s], sibling).wait_recv()
@@ -198,6 +195,22 @@
     base[...] = dot(
         jnp.concatenate([inv_hi, inv_lo, inv_hi], 0), jnp.concatenate([adj_hi, adj_hi, adj_lo], 0), ((0,), (0,))
     )
+    for shift in range(1, n_row):
+        z_copies[shift - 1].wait_recv()
+        forward(shift)
+
+    p_copies[0].wait_recv()
+    for s in range(1, n_pair):
+        slot = p_full.at[pair_from(s) * 2 + 1 - my_core]
+        remote(slot, slot, f_send.at[s], f_recv.at[s], sibling).wait_recv()
+    nt, nn = ((1,), (1,)), ((1,), (0,))
+    f_hi, f_lo = split(p_full[...].reshape(width, rows))
+    x = dot(jnp.concatenate([f_hi, f_lo], 0), t_hi[...], nn)
+    x = x[:width] + x[width:] + dot(f_hi, t_lo[...], nn)
+    x_hi, x_lo = split(x)
+    b_hi, b_lo = split(base[...])
+    d = dot(f_hi, b_hi, nt) + dot(f_hi, b_lo, nt) + dot(f_lo, b_hi, nt)
+
     inv_hi, inv_lo = split(inv_v[...].T)
     for s in range(1, n_col):
         where = cp_buf.at[col_from(s)]
@@ -209,18 +222,26 @@
     w_hi, w_lo = split(w)
     w_both = jnp.concatenate([w_hi, w_lo], 0)
 
-    q_parts, s_copies = [], []
+    s_copies, d_copies = [], []
     for h in range(chunks):
         at = slice(h * part, (h + 1) * part)
-        both = dot(w_both, t_hi[:, at], ((1,), (0,)))
-        q = base[:, at] + both[:width] + both[width:] + dot(w_hi, t_lo[:, at], ((1,), (0,)))
-        q_parts.append(q)
+        both = dot(w_both, t_hi[at, :], nt)
+        q = base[:, at] + both[:width] + both[width:] + dot(w_hi, t_lo[at, :], nt)
         by_core = q.reshape(n_pair, 2, thin, part)
         for core in range(2):
             q_buf[h, core] = by_core[:, core]
         copy = remote(q_buf.at[h, 1 - my_core], sib_in.at[h], s_send.at[h], s_recv.at[h], sibling)
         copy.start()
         s_copies.append(copy)
+        if h == 0:
+            d = -(d + dot(x_hi, w_hi, nt) + dot(x_hi, w_lo, nt) + dot(x_lo, w_hi, nt))
+            d_buf[...] = d.reshape(n_col, thin, width)
+            for s in range(1, n_col):
+                copy = remote(
+                    d_buf.at[lax.rem(my_col + s, n_col)], d_in.at[s], d_send.at[s], d_recv.at[s], col_at(s)
+                )
+                copy.start()
+                d_copies.append(copy)
 
     q_copies = []
 
@@ -236,27 +257,7 @@
             copy.start()
             q_copies.append(copy)
 
-    reduce_out(0)
-
-    p_copies[0].wait_recv()
-    for s in range(1, n_pair):
-        slot = p_full.at[pair_from(s) * 2 + 1 - my_core]
-        remote(slot, slot, f_send.at[s], f_recv.at[s], sibling).wait_recv()
-    d = jnp.zeros((width, width), jnp.float32)
-    nt = ((1,), (1,))
     for h in range(chunks):
-        q_hi, q_lo = split(q_parts[h])
-        f_hi, f_lo = split(p_full[:, :, h * part : (h + 1) * part].reshape(width, part))
-        d = d - (dot(f_hi, q_hi, nt) + dot(f_hi, q_lo, nt) + dot(f_lo, q_hi, nt))
-    d_buf[...] = d.reshape(n_col, thin, width)
-    d_copies = []
-    for s in range(1, n_col):
-        copy = remote(
-            d_buf.at[lax.rem(my_col + s, n_col)], d_in.at[s], d_send.at[s], d_recv.at[s], col_at(s)
-        )
-        copy.start()
-        d_copies.append(copy)
-    for h in range(1, chunks):
         reduce_out(h)
 
     total = d_buf[my_col]
@@ -303,7 +304,7 @@
     dma = pltpu.SemaphoreType.DMA
     grad, diag = pl.pallas_call(
         functools.partial(kernel, n_row, n_col),
-        out_shape=(jax.ShapeDtypeStruct((thin, rows), f32), jax.ShapeDtypeStruct((thin, width), f32)),
+        out_shape=(pltpu.VMEM((thin, rows), f32), pltpu.VMEM((thin, width), f32)),
         in_specs=[pl.BlockSpec(memory_space=pltpu.SMEM), hbm, hbm, hbm, hbm],
         out_specs=(vmem, vmem),
         scratch_shapes=[
@@ -311,8 +312,8 @@
             pltpu.VMEM((thin, rows), f32),
             pltpu.VMEM((thin, rows), f32),
             pltpu.VMEM((width, width), f32),
-            pltpu.VMEM((cols, rows), bf16),
-            pltpu.VMEM((cols, rows), bf16),
+            pltpu.VMEM((rows, cols), bf16),
+            pltpu.VMEM((rows, cols), bf16),
             pltpu.VMEM((width, rows), f32),
             pltpu.VMEM((n_row, thin, rows), f32),
             pltpu.VMEM((n_col, thin, rows), f32),

time: 31 us -> 28 us (0.903)
  local copies, waits for them, and re-layouts: 2.77 us -> 1.23 us
  Pallas kernels: 26.7 us -> 25.4 us
    unnamed x2, local copies, waits for them, and re-layouts: 2.77 us -> 1.23 us
    pallas_call x1, Pallas kernels: 26.7 us -> 25.4 us  [fused(): pl.pallas_call(functools.partial(kernel, n_row, n_col), out_shape=(pltpu....]
where the time goes in v5:
time: 28 us; the launch traced here: 27.9 us
  Pallas kernels  25.4 us (91%)
  between operations  1.29 us (5%)
  local copies, waits for them, and re-layouts  1.23 us (4%)
    pallas_call x1, Pallas kernels, fused(): pl.pallas_call(functools.partial(kernel, n_row, n_col), out_shape=(pltpu....  25.4 us
    unnamed x2, local copies, waits for them, and re-layouts  1.23 us

profile of v5, /device:TPU:0, one launch (start us, length us, event | category | flops | bytes accessed | tf_op | source)
XLA Modules:
  0.0 27.9 jit_solution(6634121611469677379)
XLA Ops:
  1.3 25.4 %shard_map.68 = (f32[16,1024]{1,0:T(8,128)S(1)}, f32[16,128]{1,0:T(8,128)S(1)}) custom-call(s32[1]{0:T(128)S(6)} %copy.11.idx_ref, f32[1024,512]{1,0:T(8,128)} %trail_ref.1, f32[16,1024]{1,0:T(8,128)} %bitcast.6, f32[16,1024]{1,0:T(8,128)} %bitcast.7, f32[128,128]{1,0:T(8,128)} %inv_ref.1), custom_call_target="tpu_custom_call" | custom-call | tf_op jit(solution)/shard_map/pallas_call | solution.py:305
  26.7 0.6 %copy.9 = f32[1024,16]{0,1:T(8,128)} copy(f32[1024,16]{0,1:T(8,128)S(1)} %bitcast.4) | data formatting | bytes 131072
  27.3 0.6 %copy.10 = f32[128,16]{0,1:T(8,128)} copy(f32[128,16]{0,1:T(8,128)S(1)} %bitcast.5) | data formatting | bytes 16384
